TPU v7x, 512 devices: a whole 4x8x8 slice. The times are simulated.
512 devices in a mesh: dp: 32 (over z_hi, x, core), mp: 16 (over y, z_lo).
Axes of the slice: x: 4, y: 8, z: 8 (z_hi: 4, z_lo: 2; z = z_hi * 2 + z_lo), core: 2. Of those that a mesh axis runs over, the one named last changes fastest.
Arguments:
- queries: bfloat16 [10240, 6144], P('dp', 'mp'), may hold values from -4.5 to 4.5
- key_rows: bfloat16 [10240, 6144], P('dp', 'mp'), may hold values from -4.5 to 4.5
- value_rows: bfloat16 [10240, 6144], P('dp', 'mp'), may hold values from -6 to 6
- cotangent: bfloat16 [8192, 3072], P('dp'), may hold values from -6 to 6
- out_weight: bfloat16 [6144, 3072], P('mp', 'dp'), may hold values from -0.078125 to 0.078125
- patch_counts: int32 [32, 2], replicated, may hold values from 96 to 160, as said below
- destinations: int32 [32, 2], replicated, may hold values from 0 to 31, as said below
Outputs:
- attended: bfloat16 [8192, 3072], P('dp')
- grad_queries: bfloat16 [10240, 6144], P('dp', 'mp')
- grad_keys: bfloat16 [10240, 6144], P('dp', 'mp')
- grad_values: bfloat16 [10240, 6144], P('dp', 'mp')
- grad_weight: bfloat16 [6144, 3072], P('mp', 'dp')
Inputs may be any that keep to these rules, and one draw needn't show every extreme that they name: `patch_counts`: every image has at most 160 patches; the images assigned to each device have exactly 256 patches in all; in every draw some device holds, in the loader's order, 2 images of 160 patches each. destinations[s, j] = (s - o_j) mod 32, with o_0 drawn afresh each run and o_1 = 31 - o_0; so each device receives one image of each index j.
All inputs are finite; a program needn't handle non-finite values.
Results may differ from a plain program's by a relative error of at most 0.022.
Values may be sent and summed in bfloat16 or wider, within the bound.
A program may use at most 64 MiB of HBM per device.

v0:
```python
import math

import jax
import jax.numpy as jnp
from jax import lax
from jax.sharding import PartitionSpec as P

HD = 128


def passed_along(block, axis, distance):
    devices = range(lax.axis_size(axis))
    route = [((i - distance) % len(devices), i) for i in devices]
    return lax.ppermute(block, axis, route)


def layout_tables(patch_counts, destinations):
    images = patch_counts.shape[1]
    counts = patch_counts.reshape(-1)
    targets = destinations.reshape(-1)
    serial = jnp.arange(counts.shape[0], dtype=jnp.int32)
    earlier = serial[None, :] < serial[:, None]
    same_target = targets[None, :] == targets[:, None]
    same_source = serial[None, :] // images == serial[:, None] // images
    dest_start = jnp.sum(jnp.where(earlier & same_target, counts[None, :], 0), axis=1)
    source_start = jnp.sum(jnp.where(earlier & same_source, counts[None, :], 0), axis=1)
    return (counts, targets, dest_start, source_start)


def lookup(table, index, entries):
    ids = jnp.arange(entries, dtype=jnp.int32)
    return jnp.sum(jnp.where(index[:, None] == ids[None, :], table[None, :], 0), axis=1)


def pick_rows(source, where_from, filled):
    return jnp.where(filled[:, None], source[where_from], jnp.zeros((), source.dtype))


def barrel(stacked, amounts, peers, sign, mover):
    for bit in range((peers - 1).bit_length()):
        moved = mover(stacked, sign * (1 << bit))
        taken = amounts // (1 << bit) % 2 == 1
        stacked = jnp.where(taken.reshape(-1, 1, 1), moved, stacked)
    return stacked


def attention_forward(query_heads, key_heads, value_heads, segment, scale):
    scores = (
        jnp.einsum("rhd,shd->hrs", query_heads, key_heads, preferred_element_type=jnp.float32)
        * scale
    )
    allowed = segment[:, None] == segment[None, :]
    scores = jnp.where(allowed[None], scores, -1e30)
    highest = jnp.max(scores, axis=-1, keepdims=True)
    weights = jnp.exp(scores - highest)
    softmaxed = weights / jnp.sum(weights, axis=-1, keepdims=True)
    mixed = jnp.einsum(
        "hrs,shd->rhd",
        softmaxed.astype(jnp.bfloat16),
        value_heads,
        preferred_element_type=jnp.float32,
    )
    return (mixed.astype(jnp.bfloat16), softmaxed)


def attention_backward(query_heads, key_heads, value_heads, softmaxed, grad_heads, scale):
    grad_weights = jnp.einsum(
        "rhd,shd->hrs", grad_heads, value_heads, preferred_element_type=jnp.float32
    )
    grad_value = jnp.einsum(
        "hrs,rhd->shd",
        softmaxed.astype(jnp.bfloat16),
        grad_heads,
        preferred_element_type=jnp.float32,
    ).astype(jnp.bfloat16)
    inner = jnp.sum(grad_weights * softmaxed, axis=-1, keepdims=True)
    grad_scores = (softmaxed * (grad_weights - inner) * scale).astype(jnp.bfloat16)
    grad_query = jnp.einsum(
        "hrs,shd->rhd", grad_scores, key_heads, preferred_element_type=jnp.float32
    ).astype(jnp.bfloat16)
    grad_key = jnp.einsum(
        "hrs,rhd->shd", grad_scores, query_heads, preferred_element_type=jnp.float32
    ).astype(jnp.bfloat16)
    return (grad_query, grad_key, grad_value)


def local(queries, key_rows, value_rows, cotangent, out_weight, patch_counts, destinations):
    peers = lax.axis_size("dp")
    device = lax.axis_index("dp")
    images = patch_counts.shape[1]
    source_count = queries.shape[0]
    slot_rows = source_count // images
    dest_count = cotangent.shape[0]
    width = queries.shape[1]
    heads_here = width // HD
    scale = 1.0 / math.sqrt(HD)
    contract_dims = (((1,), (1,)), ((), ()))
    counts, targets, dest_start, source_start = layout_tables(patch_counts, destinations)
    all_images = counts.shape[0]
    offsets = jnp.mod(-destinations[0], peers)
    amounts = jnp.mod(peers - offsets, peers)
    own_counts = lax.dynamic_slice_in_dim(counts, device * images, images)
    own_start = lax.dynamic_slice_in_dim(source_start, device * images, images)
    slot_ids = jnp.arange(images * slot_rows, dtype=jnp.int32)
    which = slot_ids // slot_rows
    offset = slot_ids % slot_rows
    send_filled = offset < lookup(own_counts, which, images)
    send_from = jnp.where(send_filled, lookup(own_start, which, images) + offset, 0)
    serial = jnp.arange(all_images, dtype=jnp.int32)
    dest_ids = jnp.arange(dest_count, dtype=jnp.int32)[:, None]
    arrive_match = (
        (targets[None, :] == device)
        & (dest_ids >= dest_start[None, :])
        & (dest_ids < dest_start[None, :] + counts[None, :])
    )
    arrive_pos = serial[None, :] % images * slot_rows + dest_ids - dest_start[None, :]
    arrive_from = jnp.sum(jnp.where(arrive_match, arrive_pos, 0), axis=1)
    arrive_segment = jnp.sum(jnp.where(arrive_match, serial[None, :], 0), axis=1)
    sender = jnp.mod(device + lookup(offsets, which, images), peers)
    sender_image = sender * images + which
    back_filled = offset < lookup(counts, sender_image, all_images)
    back_from = jnp.where(back_filled, lookup(dest_start, sender_image, all_images) + offset, 0)
    home_ids = jnp.arange(source_count, dtype=jnp.int32)[:, None]
    image_ids = jnp.arange(images, dtype=jnp.int32)[None, :]
    home_match = (home_ids >= own_start[None, :]) & (
        home_ids < own_start[None, :] + own_counts[None, :]
    )
    home_from = jnp.sum(
        jnp.where(home_match, image_ids * slot_rows + home_ids - own_start[None, :], 0), axis=1
    )
    home_live = jnp.any(home_match, axis=1)

    def split_heads(rows):
        return rows.reshape(rows.shape[0], heads_here, HD)

    outgoing = jnp.stack(
        [
            pick_rows(queries, send_from, send_filled),
            pick_rows(key_rows, send_from, send_filled),
            pick_rows(value_rows, send_from, send_filled),
        ]
    )
    arrived = barrel(
        outgoing.reshape(3, images, slot_rows, width),
        amounts,
        peers,
        1,
        lambda stacked, by: passed_along(stacked, "dp", by),
    )
    arrived = arrived.reshape(3, images * slot_rows, width)
    query_heads = split_heads(arrived[0][arrive_from])
    key_heads = split_heads(arrived[1][arrive_from])
    value_heads = split_heads(arrived[2][arrive_from])
    mixed_heads, softmaxed = attention_forward(
        query_heads, key_heads, value_heads, arrive_segment, scale
    )
    mixed_rows = mixed_heads.reshape(dest_count, width)
    full_weight = lax.all_gather(out_weight, "dp", axis=1, tiled=True)
    partial_value = jnp.dot(mixed_rows, full_weight, preferred_element_type=jnp.float32)
    attended = lax.psum(partial_value.astype(jnp.bfloat16), "mp")
    grad_mixed = lax.dot_general(
        cotangent, full_weight, contract_dims, preferred_element_type=jnp.float32
    ).astype(jnp.bfloat16)
    weight_term = lax.dot_general(
        mixed_rows, cotangent, (((0,), (0,)), ((), ())), preferred_element_type=jnp.float32
    )
    grad_weight = lax.psum_scatter(
        weight_term.astype(jnp.bfloat16), "dp", scatter_dimension=1, tiled=True
    )
    grad_query, grad_key, grad_value = attention_backward(
        query_heads, key_heads, value_heads, softmaxed, split_heads(grad_mixed), scale
    )
    returned = jnp.stack(
        [
            pick_rows(grad_query.reshape(dest_count, width), back_from, back_filled),
            pick_rows(grad_key.reshape(dest_count, width), back_from, back_filled),
            pick_rows(grad_value.reshape(dest_count, width), back_from, back_filled),
        ]
    )
    homed = barrel(
        returned.reshape(3, images, slot_rows, width),
        amounts,
        peers,
        -1,
        lambda stacked, by: passed_along(stacked, "dp", by),
    )
    homed = homed.reshape(3, images * slot_rows, width)
    grad_queries = pick_rows(homed[0], home_from, home_live)
    grad_keys = pick_rows(homed[1], home_from, home_live)
    grad_values = pick_rows(homed[2], home_from, home_live)
    return (attended, grad_queries, grad_keys, grad_values, grad_weight)


def solution(mesh):
    in_specs = (P("dp", "mp"), P("dp", "mp"), P("dp", "mp"), P("dp", None), P("mp", "dp"), P(), P())
    out_specs = (P("dp", None), P("dp", "mp"), P("dp", "mp"), P("dp", "mp"), P("mp", "dp"))
    return jax.shard_map(local, mesh=mesh, in_specs=in_specs, out_specs=out_specs, check_vma=False)
```

profile of v0, /device:TPU:16, one launch (start us, length us, event | category | flops | bytes accessed | tf_op | source)
XLA Modules:
  0.0 562.5 jit_solution(14568119585027243148)
XLA Ops:
  7.3 0.9 copy.47
  8.2 0.8 fusion.32
  9.0 0.8 copy.46
  10.0 0.2 select_reduce_fusion.4
  10.5 2.9 gather_fusion
  13.4 2.0 gather_fusion.1
  15.5 2.0 gather_fusion.2
  17.6 0.2 broadcast_select_fusion.18
  17.8 1.9 collective-permute-start
  19.8 19.9 %collective-permute-done = bf16[3,2,160,384]{3,2,1,0:T(8,128)(2,1)S(1)} collective-permute-done((bf16[3,2,160,384]{3,2,1,0:T(8,128)(2,1)S(1)}, bf16[3,2,160,384]{3,2,1,0:T(8,128)(2,1)S(1)}, u32[]{:S(2)}, u32[]{:S(2)}) %collective-permute-start) | collective-permute-done | bytes 737312 | tf_op jit(solution)/shard_map/ppermute | solution.py:14
  39.7 1.0 broadcast_select_fusion.1
  40.7 1.9 collective-permute-start.1
  42.7 44.7 %collective-permute-done.1 = bf16[3,2,160,384]{3,2,1,0:T(8,128)(2,1)} collective-permute-done((bf16[3,2,160,384]{3,2,1,0:T(8,128)(2,1)}, bf16[3,2,160,384]{3,2,1,0:T(8,128)(2,1)}, u32[]{:S(2)}, u32[]{:S(2)}) %collective-permute-start.1) | collective-permute-done | bytes 737312 | tf_op jit(solution)/shard_map/ppermute | solution.py:14
  87.4 1.3 broadcast_select_fusion.3
  88.7 1.9 collective-permute-start.2
  90.7 38.7 %collective-permute-done.2 = bf16[3,2,160,384]{3,2,1,0:T(8,128)(2,1)S(1)} collective-permute-done((bf16[3,2,160,384]{3,2,1,0:T(8,128)(2,1)S(1)}, bf16[3,2,160,384]{3,2,1,0:T(8,128)(2,1)S(1)}, u32[]{:S(2)}, u32[]{:S(2)}) %collective-permute-start.2) | collective-permute-done | bytes 737312 | tf_op jit(solution)/shard_map/ppermute | solution.py:14
  129.3 0.2 broadcast_select_fusion.5
  129.5 1.9 collective-permute-start.3
  131.6 24.8 %collective-permute-done.3 = bf16[3,2,160,384]{3,2,1,0:T(8,128)(2,1)S(1)} collective-permute-done((bf16[3,2,160,384]{3,2,1,0:T(8,128)(2,1)S(1)}, bf16[3,2,160,384]{3,2,1,0:T(8,128)(2,1)S(1)}, u32[]{:S(2)}, u32[]{:S(2)}) %collective-permute-start.3) | collective-permute-done | bytes 737312 | tf_op jit(solution)/shard_map/ppermute | solution.py:14
  156.4 0.2 broadcast_select_fusion.7
  156.6 35.3 %collective-permute-start.4 = (bf16[3,2,160,384]{3,2,1,0:T(8,128)(2,1)S(1)}, bf16[3,2,160,384]{3,2,1,0:T(8,128)(2,1)S(1)}, u32[]{:S(2)}, u32[]{:S(2)}) collective-permute-start(bf16[3,2,160,384]{3,2,1,0:T(8,128)(2,1)S(1)} %broadcast_select_fusion.7), channel_id=1, source_target_pairs={{256,0},{272,16},{288,32},{304,48},{320,64},{336,80},{352,96},{368... | collective-permute-start | bytes 2211848 | tf_op jit(solution)/shard_map/ppermute | solution.py:14
  192.3 16.3 %collective-permute-done.4 = bf16[3,2,160,384]{3,2,1,0:T(8,128)(2,1)S(1)} collective-permute-done((bf16[3,2,160,384]{3,2,1,0:T(8,128)(2,1)S(1)}, bf16[3,2,160,384]{3,2,1,0:T(8,128)(2,1)S(1)}, u32[]{:S(2)}, u32[]{:S(2)}) %collective-permute-start.4) | collective-permute-done | bytes 737312 | tf_op jit(solution)/shard_map/ppermute | solution.py:14
  208.7 0.2 broadcast_select_fusion.9
  208.9 1.2 gather_fusion.5
  210.2 1.2 gather_fusion.4
  211.5 1.2 gather_fusion.3
  212.9 1.3 fusion.57
  214.2 2.6 convolution_convert_fusion.2
  217.0 0.6 convolution_convert_fusion.3
  217.6 0.3 fusion.58
  218.0 1.8 convolution_convert_fusion.4
  219.8 1.8 convolution_convert_fusion.5
  221.6 0.2 copy.62
  221.8 0.2 copy.60
  222.0 2.0 gather_fusion.8
  224.0 2.0 gather_fusion.7
  226.1 0.2 copy.58
  226.3 2.0 gather_fusion.6
  228.3 0.2 broadcast_select_fusion.15
  228.5 1.0 pad_maximum_fusion.1
  229.4 1.9 collective-permute-start.5
  231.4 1.6 convolution_convert_fusion.6
  233.0 3.8 convolution_convert_fusion.1
  236.9 3.8 collective-permute-done.5
  240.7 0.2 broadcast_select_fusion
  240.9 1.9 collective-permute-start.6
  242.8 25.7 %collective-permute-done.6 = bf16[3,2,160,384]{3,2,1,0:T(8,128)(2,1)S(1)} collective-permute-done((bf16[3,2,160,384]{3,2,1,0:T(8,128)(2,1)S(1)}, bf16[3,2,160,384]{3,2,1,0:T(8,128)(2,1)S(1)}, u32[]{:S(2)}, u32[]{:S(2)}) %collective-permute-start.6) | collective-permute-done | bytes 737312 | tf_op jit(solution)/shard_map/ppermute | solution.py:14
  268.5 1.1 broadcast_select_fusion.2
  269.5 1.9 collective-permute-start.7
  271.4 2.4 convolution_convert_fusion
  273.9 18.3 %collective-permute-done.7 = bf16[3,2,160,384]{3,2,1,0:T(8,128)(2,1)S(1)} collective-permute-done((bf16[3,2,160,384]{3,2,1,0:T(8,128)(2,1)}, bf16[3,2,160,384]{3,2,1,0:T(8,128)(2,1)S(1)}, u32[]{:S(2)}, u32[]{:S(2)}) %collective-permute-start.7) | collective-permute-done | bytes 737312 | tf_op jit(solution)/shard_map/ppermute | solution.py:14
  292.2 1.3 broadcast_select_fusion.4
  293.4 1.9 collective-permute-start.8
  295.4 22.6 %collective-permute-done.8 = bf16[3,2,160,384]{3,2,1,0:T(8,128)(2,1)S(1)} collective-permute-done((bf16[3,2,160,384]{3,2,1,0:T(8,128)(2,1)S(1)}, bf16[3,2,160,384]{3,2,1,0:T(8,128)(2,1)S(1)}, u32[]{:S(2)}, u32[]{:S(2)}) %collective-permute-start.8) | collective-permute-done | bytes 737312 | tf_op jit(solution)/shard_map/ppermute | solution.py:14
  318.1 4.8 collective-permute-start.9
  323.0 53.6 %collective-permute-done.9 = bf16[3,2,160,384]{3,2,1,0:T(8,128)(2,1)S(1)} collective-permute-done((bf16[3,2,160,384]{3,2,1,0:T(8,128)(2,1)S(1)}, bf16[3,2,160,384]{3,2,1,0:T(8,128)(2,1)S(1)}, u32[]{:S(2)}, u32[]{:S(2)}) %collective-permute-start.9) | collective-permute-done | bytes 737312 | tf_op jit(solution)/shard_map/ppermute | solution.py:14
  376.6 0.2 broadcast_select_fusion.8
  376.8 2.0 gather_fusion.10
  378.9 2.0 gather_fusion.9
  381.0 2.0 gather_fusion.11
  383.0 1.0 broadcast_select_fusion.10
  384.0 57.7 %all-reduce.2.cloned.1.call-done = bf16[256,3072]{1,0:T(8,128)(2,1)} async-done(((bf16[256,3072]{1,0:T(8,128)(2,1)}), bf16[256,3072]{1,0:T(8,128)(2,1)}) %all-reduce.2.cloned.1.call-update) | async-done | bytes 1572880 | tf_op jit(solution)/shard_map/psum | solution.py:160
  441.7 111.6 %reduce-scatter.2.cloned.1.call-done = bf16[384,96]{0,1:T(8,128)(2,1)} async-done(((bf16[384,3072]{0,1:T(8,128)(2,1)}), bf16[384,96]{0,1:T(8,128)(2,1)}) %reduce-scatter.2.cloned.1.call-update) | async-done | bytes 73744 | tf_op jit(solution)/shard_map/reduce_scatter | solution.py:167
  553.3 2.7 copy.72
  (53 shorter events, 2.4 us)
Async XLA Ops:
  7.2 207.0 %copy-start = (bf16[256,3072]{1,0:T(8,128)(2,1)S(1)}, bf16[256,3072]{1,0:T(8,128)(2,1)}, u32[]{:S(2)}) copy-start(bf16[256,3072]{1,0:T(8,128)(2,1)} %param.10) | copy-start | bytes 4718596
  7.2 6.2 %copy-start.1 = (bf16[320,384]{1,0:T(8,128)(2,1)S(1)}, bf16[320,384]{1,0:T(8,128)(2,1)}, u32[]{:S(2)}) copy-start(bf16[320,384]{1,0:T(8,128)(2,1)} %param.8) | copy-start | bytes 737284
  7.2 8.3 %copy-start.2 = (bf16[320,384]{1,0:T(8,128)(2,1)S(1)}, bf16[320,384]{1,0:T(8,128)(2,1)}, u32[]{:S(2)}) copy-start(bf16[320,384]{1,0:T(8,128)(2,1)} %param.9) | copy-start | bytes 737284
  7.2 207.0 %all-gather.2.cloned.1.call-start = ((), (), s32[]{:S(2)}) async-start(), calls=%async_computation.1 | async-start | bytes 2433024 | tf_op jit(solution)/shard_map/all_gather | solution.py:158
  17.8 21.9 %collective-permute-start = (bf16[3,2,160,384]{3,2,1,0:T(8,128)(2,1)S(1)}, bf16[3,2,160,384]{3,2,1,0:T(8,128)(2,1)S(1)}, u32[]{:S(2)}, u32[]{:S(2)}) collective-permute-start(bf16[3,2,160,384]{3,2,1,0:T(8,128)(2,1)S(1)} %pad_maximum_fusion), channel_id=1, source_target_pairs={{496,0},{0,16},{16,32},{32,48},{48,64},{64,80},{80,96},{96,112},{1... | collective-permute-start | bytes 2211848 | tf_op jit(solution)/shard_map/ppermute | solution.py:14
  40.7 46.7 %collective-permute-start.1 = (bf16[3,2,160,384]{3,2,1,0:T(8,128)(2,1)}, bf16[3,2,160,384]{3,2,1,0:T(8,128)(2,1)}, u32[]{:S(2)}, u32[]{:S(2)}) collective-permute-start(bf16[3,2,160,384]{3,2,1,0:T(8,128)(2,1)} %broadcast_select_fusion.1), channel_id=1, source_target_pairs={{480,0},{496,16},{0,32},{16,48},{32,64},{48,80},{64,96},{80,112},{... | collective-permute-start | bytes 2211848 | tf_op jit(solution)/shard_map/ppermute | solution.py:14
  42.7 399.0 %all-reduce.2.cloned.1.call-start = ((), (), s32[]{:S(2)}) async-start(), calls=%async_computation.2 | async-start | bytes 3145728 | tf_op jit(solution)/shard_map/psum | solution.py:160
  88.7 40.6 %collective-permute-start.2 = (bf16[3,2,160,384]{3,2,1,0:T(8,128)(2,1)S(1)}, bf16[3,2,160,384]{3,2,1,0:T(8,128)(2,1)S(1)}, u32[]{:S(2)}, u32[]{:S(2)}) collective-permute-start(bf16[3,2,160,384]{3,2,1,0:T(8,128)(2,1)S(1)} %broadcast_select_fusion.3), channel_id=1, source_target_pairs={{448,0},{464,16},{480,32},{496,48},{0,64},{16,80},{32,96},{48,112}... | collective-permute-start | bytes 2211848 | tf_op jit(solution)/shard_map/ppermute | solution.py:14
  129.5 26.9 %collective-permute-start.3 = (bf16[3,2,160,384]{3,2,1,0:T(8,128)(2,1)S(1)}, bf16[3,2,160,384]{3,2,1,0:T(8,128)(2,1)S(1)}, u32[]{:S(2)}, u32[]{:S(2)}) collective-permute-start(bf16[3,2,160,384]{3,2,1,0:T(8,128)(2,1)S(1)} %broadcast_select_fusion.5), channel_id=1, source_target_pairs={{384,0},{400,16},{416,32},{432,48},{448,64},{464,80},{480,96},{496... | collective-permute-start | bytes 2211848 | tf_op jit(solution)/shard_map/ppermute | solution.py:14
  156.6 52.1 %collective-permute-start.4 = (bf16[3,2,160,384]{3,2,1,0:T(8,128)(2,1)S(1)}, bf16[3,2,160,384]{3,2,1,0:T(8,128)(2,1)S(1)}, u32[]{:S(2)}, u32[]{:S(2)}) collective-permute-start(bf16[3,2,160,384]{3,2,1,0:T(8,128)(2,1)S(1)} %broadcast_select_fusion.7), channel_id=1, source_target_pairs={{256,0},{272,16},{288,32},{304,48},{320,64},{336,80},{352,96},{368... | collective-permute-start | bytes 2211848 | tf_op jit(solution)/shard_map/ppermute | solution.py:14
  210.2 9.6 %copy-start.3 = (bf16[256,384]{0,1:T(8,128)(2,1)}, bf16[256,384]{0,1:T(8,128)(2,1)S(1)}, u32[]{:S(2)}) copy-start(bf16[256,384]{0,1:T(8,128)(2,1)S(1)} %copy.50) | copy-start | bytes 589828
  211.5 6.4 %copy-start.4 = (bf16[256,384]{0,1:T(8,128)(2,1)}, bf16[256,384]{0,1:T(8,128)(2,1)S(1)}, u32[]{:S(2)}) copy-start(bf16[256,384]{0,1:T(8,128)(2,1)S(1)} %copy.49) | copy-start | bytes 589828
  229.4 11.2 %collective-permute-start.5 = (bf16[3,2,160,384]{3,2,1,0:T(8,128)(2,1)}, bf16[3,2,160,384]{3,2,1,0:T(8,128)(2,1)S(1)}, u32[]{:S(2)}, u32[]{:S(2)}) collective-permute-start(bf16[3,2,160,384]{3,2,1,0:T(8,128)(2,1)} %pad_maximum_fusion.1), channel_id=1, source_target_pairs={{16,0},{32,16},{48,32},{64,48},{80,64},{96,80},{112,96},{128,112},... | collective-permute-start | bytes 2211848 | tf_op jit(solution)/shard_map/ppermute | solution.py:14
  236.9 316.4 %reduce-scatter.2.cloned.1.call-start = ((), (), s32[]{:S(2)}) async-start(), calls=%async_computation.3 | async-start | bytes 2433024 | tf_op jit(solution)/shard_map/reduce_scatter | solution.py:167
  240.9 27.6 %collective-permute-start.6 = (bf16[3,2,160,384]{3,2,1,0:T(8,128)(2,1)S(1)}, bf16[3,2,160,384]{3,2,1,0:T(8,128)(2,1)S(1)}, u32[]{:S(2)}, u32[]{:S(2)}) collective-permute-start(bf16[3,2,160,384]{3,2,1,0:T(8,128)(2,1)S(1)} %broadcast_select_fusion), channel_id=1, source_target_pairs={{32,0},{48,16},{64,32},{80,48},{96,64},{112,80},{128,96},{144,112}... | collective-permute-start | bytes 2211848 | tf_op jit(solution)/shard_map/ppermute | solution.py:14
  269.5 22.6 %collective-permute-start.7 = (bf16[3,2,160,384]{3,2,1,0:T(8,128)(2,1)}, bf16[3,2,160,384]{3,2,1,0:T(8,128)(2,1)S(1)}, u32[]{:S(2)}, u32[]{:S(2)}) collective-permute-start(bf16[3,2,160,384]{3,2,1,0:T(8,128)(2,1)} %broadcast_select_fusion.2), channel_id=1, source_target_pairs={{64,0},{80,16},{96,32},{112,48},{128,64},{144,80},{160,96},{176,11... | collective-permute-start | bytes 2211848 | tf_op jit(solution)/shard_map/ppermute | solution.py:14
  293.4 24.5 %collective-permute-start.8 = (bf16[3,2,160,384]{3,2,1,0:T(8,128)(2,1)S(1)}, bf16[3,2,160,384]{3,2,1,0:T(8,128)(2,1)S(1)}, u32[]{:S(2)}, u32[]{:S(2)}) collective-permute-start(bf16[3,2,160,384]{3,2,1,0:T(8,128)(2,1)S(1)} %broadcast_select_fusion.4), channel_id=1, source_target_pairs={{128,0},{144,16},{160,32},{176,48},{192,64},{208,80},{224,96},{240... | collective-permute-start | bytes 2211848 | tf_op jit(solution)/shard_map/ppermute | solution.py:14
  318.1 58.5 %collective-permute-start.9 = (bf16[3,2,160,384]{3,2,1,0:T(8,128)(2,1)S(1)}, bf16[3,2,160,384]{3,2,1,0:T(8,128)(2,1)S(1)}, u32[]{:S(2)}, u32[]{:S(2)}) collective-permute-start(bf16[3,2,160,384]{3,2,1,0:T(8,128)(2,1)S(1)} %broadcast_select_fusion.6), channel_id=1, source_target_pairs={{256,0},{272,16},{288,32},{304,48},{320,64},{336,80},{352,96},{368... | collective-permute-start | bytes 2211848 | tf_op jit(solution)/shard_map/ppermute | solution.py:14
Sparse Core Ops, SparseCore 0:
  42.8 89.9 all-gather.1
  237.0 204.6 all-reduce.1
  447.4 105.8 reduce-scatter.1
where the time goes:
time: 563 us; the launch traced here: 562 us
  waiting for transfers between devices  438 us (78%)
  starting transfers between devices  55.6 us (10%)
  local copies, waits for them, and re-layouts  28.7 us (5%)
  matrix products  16.5 us (3%)
  between operations  14.2 us (3%)
  other arithmetic  9.87 us (2%)
    ppermute x10, waiting for transfers between devices, passed_along(): return lax.ppermute(block, axis, route)  268 us
    reduce_scatter x1, waiting for transfers between devices, local(): lax.psum_scatter(weight_term.astype(jnp.bfloat16), 'dp', scatter_dimensio...  112 us
    psum x1, waiting for transfers between devices, local(): attended = lax.psum(partial_value.astype(jnp.bfloat16), 'mp')  57.7 us
    ppermute x10, starting transfers between devices, passed_along(): return lax.ppermute(block, axis, route)  55.5 us
    gather x9, local copies, waits for them, and re-layouts, pick_rows(): source[where_from]  19.3 us
  transfers between devices with their start and end apart: 13, of which 12 were waited for; matrix products, arithmetic and copies ran while one was open for 5% of the time, Pallas kernels for 0%

commit v1 on v0

v1 whole, which is shorter than its diff:
```python
import functools
import math

import jax
import jax.numpy as jnp
from jax import lax
from jax.experimental import pallas as pl
from jax.experimental.pallas import tpu as pltpu
from jax.sharding import PartitionSpec as P

HD = 128
HEADS = 3
NDP = 32
SLOT = 160
ROWS = 320
DEST = 256
FEAT = 96
WIDTH = HEADS * HD
OUT = 3072
HALF = OUT // 2
SCALE = 1.0 / math.sqrt(HD)
MESH = pl.DeviceIdType.MESH
F32 = jnp.float32
BF16 = jnp.bfloat16


def dot(a, b, dims):
    return lax.dot_general(a, b, (dims, ((), ())), preferred_element_type=F32)


def place():
    dp = lax.axis_index("dp")
    mp = lax.axis_index("mp")
    return dp, mp, dp // 8, (dp // 2) % 4, dp % 2, mp // 2, mp % 2


def dp_of(zh, x, core):
    return (zh * 4 + x) * 2 + core


def mod(a, n):
    return lax.rem(a + n, n)


def remote(src, dst, ss, rs, dp, mp):
    return pltpu.make_async_remote_copy(
        src_ref=src, dst_ref=dst, send_sem=ss, recv_sem=rs, device_id=(dp, mp), device_id_type=MESH
    )


def greet(peers):
    barrier = pltpu.get_barrier_semaphore()
    for dp, mp in peers:
        pl.semaphore_signal(barrier, inc=1, device_id=(dp, mp), device_id_type=MESH)


def greeted(count):
    pl.semaphore_wait(pltpu.get_barrier_semaphore(), count)


def tables(counts_ref, dests_ref, dp):
    o0 = mod(-dests_ref[0, 0], NDP)
    swap = (o0 >= NDP // 2).astype(jnp.int32)
    turn = jnp.where(swap == 1, NDP - 1 - o0, o0)
    c0 = counts_ref[dp, 0]
    c1 = counts_ref[dp, 1]
    home = (
        (jnp.where(swap == 1, c0, 0), jnp.where(swap == 1, c1, c0)),
        (jnp.where(swap == 1, 0, c0), jnp.where(swap == 1, c0, c1)),
    )
    src_a = lax.rem(dp + turn, NDP)
    src_b = mod(dp - turn - 1, NDP)
    count_a = counts_ref[src_a, swap]
    count_b = counts_ref[src_b, 1 - swap]
    a_first = src_a < src_b
    dest = (
        (jnp.where(a_first, 0, count_b), count_a),
        (jnp.where(a_first, count_a, 0), count_b),
    )
    return home, dest, (c0, c0 + c1)


def iota(shape, dim):
    return lax.broadcasted_iota(jnp.int32, shape, dim)


def pick(rows, start, count):
    shape = (SLOT, rows)
    r, c = iota(shape, 0), iota(shape, 1)
    return jnp.where((c == r + start) & (r < count), 1.0, 0.0).astype(BF16)


def put(rows, start, count):
    shape = (rows, SLOT)
    r, c = iota(shape, 0), iota(shape, 1)
    return jnp.where((r == c + start) & (c < count), 1.0, 0.0).astype(BF16)


def allowed(bounds):
    first, last = bounds

    def segment(shape, dim):
        ids = iota(shape, dim)
        return jnp.where(ids < first, 0, jnp.where(ids < last, 1, 2))

    return segment((ROWS, ROWS), 0) == segment((ROWS, ROWS), 1)


def probabilities(q, k, mask):
    scores = dot(q, k, ((1,), (1,))) * SCALE
    scores = jnp.where(mask, scores, -1e30)
    weights = jnp.exp(scores - jnp.max(scores, axis=-1, keepdims=True))
    return weights / jnp.sum(weights, axis=-1, keepdims=True)


def first_kernel(counts_ref, dests_ref, q_ref, k_ref, v_ref, cot_ref, w_ref, slots_ref, wt_ref, mixed_ref, ss, rs):
    dp, mp, zh, x, core, y, zl = place()
    sibling = dp_of(zh, x, 1 - core)
    xs = [dp_of(zh, lax.rem(x + i, 4), core) for i in (1, 3, 2)]
    zs = [dp_of(lax.rem(zh + i, 4), x, core) for i in (1, 3, 2)]
    peers = [sibling] + xs + zs
    greet([(p, mp) for p in peers])
    home, dest, bounds = tables(counts_ref, dests_ref, dp)
    wt_ref[dp] = jnp.transpose(w_ref[...].astype(F32)).astype(BF16)
    greeted(len(peers))
    sends = []

    def send(shard, to):
        i = len(sends)
        copy = remote(wt_ref.at[shard], wt_ref.at[shard], ss.at[i], rs.at[shard], to, mp)
        copy.start()
        sends.append(copy)

    def arrive(shard):
        remote(wt_ref.at[shard], wt_ref.at[shard], ss.at[0], rs.at[shard], dp, mp).wait_recv()

    for p in zs + xs + [sibling]:
        send(dp, p)
    mask = allowed(bounds)

    def head(h):
        cols = slice(h * HD, (h + 1) * HD)
        probs = probabilities(q_ref[:, cols], k_ref[:, cols], mask)
        mixed_ref[:, cols] = dot(probs.astype(BF16), v_ref[:, cols], ((1,), (0,))).astype(BF16)

    head(0)
    for i in (1, 3, 2):
        z = lax.rem(zh + i, 4)
        shard = dp_of(z, x, core)
        arrive(shard)
        for p in xs:
            send(shard, p)
        send(shard, sibling)
    head(1)
    for shard in xs:
        arrive(shard)
        send(shard, sibling)
    head(2)
    for slot in range(2):
        start, count = home[slot]
        slots_ref[slot] = dot(pick(ROWS, start, count), mixed_ref[...], ((1,), (0,))).astype(BF16)
    for i in (1, 3, 2):
        for j in (1, 3, 2):
            shard = dp_of(lax.rem(zh + i, 4), lax.rem(x + j, 4), core)
            arrive(shard)
            send(shard, sibling)
    for i in range(4):
        for j in range(4):
            arrive(dp_of(lax.rem(zh + i, 4), lax.rem(x + j, 4), 1 - core))
    grad = dot(cot_ref[...], wt_ref[...].reshape(OUT, WIDTH), ((1,), (0,))).astype(BF16)
    for slot in range(2):
        start, count = dest[slot]
        slots_ref[2 + slot] = dot(pick(DEST, start, count), grad, ((1,), (0,))).astype(BF16)
    for copy in sends:
        copy.wait_send()


def turn_kernel(turn, in_ref, out_ref, ss, rs):
    dp, mp, *_ = place()
    back_a, on_a = mod(dp - turn, NDP), lax.rem(dp + turn, NDP)
    on_b, back_b = lax.rem(dp + turn + 1, NDP), mod(dp - turn - 1, NDP)
    routes = [(0, back_a), (1, on_b), (2, on_a), (3, back_b)]
    if turn == 0:
        others = [routes[1], routes[3]]
        own = [routes[0], routes[2]]
    else:
        others, own = routes, []
    greet([(p, mp) for _, p in others])
    local = [pltpu.make_async_copy(in_ref.at[i], out_ref.at[i], ss.at[i]) for i, _ in own]
    for copy in local:
        copy.start()
    greeted(len(others))
    copies = [remote(in_ref.at[i], out_ref.at[i], ss.at[i], rs.at[i], p, mp) for i, p in others]
    for copy in copies:
        copy.start()
    for copy in local + copies:
        copy.wait()


def second_kernel(
    counts_ref, dests_ref, in_ref, q_ref, k_ref, v_ref, cot_ref, wt_ref,
    att_ref, gq_ref, gk_ref, gv_ref, gw_ref,
    mixed_ref, part_ref, ring_ref, fold_ref, term_ref, core_ref, xin_ref, zin_ref, gm_ref,
    ring_s, ring_r, fold_s, fold_r, gath_s, gath_r, red_s, red_r,
):
    dp, mp, zh, x, core, y, zl = place()
    mp_of = lambda yy, zz: yy * 2 + zz
    up, down = mp_of(lax.rem(y + 1, 8), zl), mp_of(lax.rem(y + 7, 8), zl)
    across = mp_of(y, 1 - zl)
    sibling = dp_of(zh, x, 1 - core)
    xs = [dp_of(zh, lax.rem(x + i, 4), core) for i in (1, 3, 2)]
    zs = [dp_of(lax.rem(zh + i, 4), x, core) for i in (1, 3, 2)]
    greet([(dp, up), (dp, down), (dp, across)] + [(p, mp) for p in [sibling] + xs + zs])
    home, dest, bounds = tables(counts_ref, dests_ref, dp)
    mixed_ref[...] = (
        dot(put(DEST, *dest[0]), in_ref[0], ((1,), (0,))) + dot(put(DEST, *dest[1]), in_ref[1], ((1,), (0,)))
    ).astype(BF16)
    for c in range(8):
        cols = slice(c * WIDTH, (c + 1) * WIDTH)
        w = wt_ref[4 * c : 4 * c + 4].reshape(WIDTH, WIDTH)
        part_ref[:, cols] = dot(mixed_ref[...], w, ((1,), (1,))).astype(BF16)
    greeted(10)

    def chunk(ref, yy, sub):
        rows = pl.ds(pl.multiple_of(yy * 32, 32), 32)
        return ref.at[rows, pl.ds(sub * HALF, HALF)]

    pending = []

    def ring_copy(way, step, sub):
        to = up if way == 0 else down
        yy = lax.rem(y + 4 - step, 8) if way == 0 else lax.rem(y + 4 + step, 8)
        return remote(
            chunk(part_ref, yy, sub), ring_ref.at[way, step, sub], ring_s.at[way, step, sub],
            ring_r.at[way, step, sub], dp, to,
        )

    def ring_send(way, step, sub):
        copy = ring_copy(way, step, sub)
        copy.start()
        pending.append(copy)

    def ring_take(way, step, sub):
        ring_copy(way, step, sub).wait_recv()
        yy = lax.rem(y + 3 - step, 8) if way == 0 else lax.rem(y + 5 + step, 8)
        ref = chunk(part_ref, yy, sub)
        ref[...] = (ref[...].astype(F32) + ring_ref[way, step, sub].astype(F32)).astype(BF16)

    ring_send(0, 0, 0)
    ring_send(1, 0, 1)
    ring_send(0, 1, 1)
    ring_send(1, 1, 0)

    for c in range(8):
        cols = slice(c * WIDTH, (c + 1) * WIDTH)
        block = dot(cot_ref[:, cols], mixed_ref[...], ((0,), (0,))).astype(BF16)
        for i in range(4):
            j = 4 * c + i
            term_ref[j % 2, (j // 2) % 4, j // 8] = block[i * FEAT : (i + 1) * FEAT]
    swap = remote(term_ref.at[1 - core], core_ref, red_s.at[0], red_r.at[0], sibling, mp)
    swap.start()

    ring_take(0, 0, 0)
    ring_send(0, 1, 0)
    ring_take(1, 0, 1)
    ring_send(1, 1, 1)

    swap.wait_recv()
    term_ref[core] = (term_ref[core].astype(F32) + core_ref[...].astype(F32)).astype(BF16)
    xcopies = []
    for n, i in enumerate((1, 3, 2)):
        copy = remote(
            term_ref.at[core, lax.rem(x + i, 4)], xin_ref.at[n], red_s.at[1 + n], red_r.at[1 + n], xs[n], mp
        )
        copy.start()
        xcopies.append(copy)

    for step in (1, 2):
        for way, sub in ((0, 1), (1, 0), (0, 0), (1, 1)):
            ring_take(way, step, sub)
            ring_send(way, step + 1, sub)

    for copy in xcopies:
        copy.wait_recv()
    total = term_ref[core, x].astype(F32)
    for n in range(3):
        total = total + xin_ref[n].astype(F32)
    term_ref[core, x] = total.astype(BF16)
    zcopies = []
    for n, i in enumerate((1, 3, 2)):
        copy = remote(
            term_ref.at[core, x, lax.rem(zh + i, 4)], zin_ref.at[n], red_s.at[4 + n], red_r.at[4 + n], zs[n], mp
        )
        copy.start()
        zcopies.append(copy)

    folds = []
    for way, sub in ((0, 1), (0, 0)):
        other = 1 - way
        ring_copy(way, 3, sub).wait_recv()
        ring_copy(other, 3, sub).wait_recv()
        ref = chunk(part_ref, y, sub)
        ref[...] = (
            ref[...].astype(F32) + ring_ref[way, 3, sub].astype(F32) + ring_ref[other, 3, sub].astype(F32)
        ).astype(BF16)
        copy = remote(ref, fold_ref.at[sub], fold_s.at[sub], fold_r.at[sub], dp, across)
        copy.start()
        folds.append((sub, copy))

    def gather_copy(way, step, sub):
        to = up if way == 0 else down
        yy = mod(y - step, 8) if way == 0 else lax.rem(y + step, 8)
        return remote(
            chunk(att_ref, yy, sub), chunk(att_ref, yy, sub), gath_s.at[way, step, sub],
            gath_r.at[way, step, sub], dp, to,
        )

    def gather_send(way, step, sub):
        copy = gather_copy(way, step, sub)
        copy.start()
        pending.append(copy)

    def gather_take(way, step, sub):
        to = up if way == 0 else down
        yy = mod(y - step - 1, 8) if way == 0 else lax.rem(y + step + 1, 8)
        remote(
            chunk(att_ref, yy, sub), chunk(att_ref, yy, sub), gath_s.at[way, step, sub],
            gath_r.at[way, step, sub], dp, to,
        ).wait_recv()

    for sub, copy in folds:
        copy.wait_recv()
        mine = chunk(part_ref, y, sub)
        chunk(att_ref, y, sub)[...] = (mine[...].astype(F32) + fold_ref[sub].astype(F32)).astype(BF16)
        gather_send(0, 0, sub)
        gather_send(1, 0, sub)

    gm_ref[...] = (
        dot(put(ROWS, *home[0]), in_ref[2], ((1,), (0,))) + dot(put(ROWS, *home[1]), in_ref[3], ((1,), (0,)))
    ).astype(BF16)
    mask = allowed(bounds)

    def head(h):
        cols = slice(h * HD, (h + 1) * HD)
        q, k, v, gm = q_ref[:, cols], k_ref[:, cols], v_ref[:, cols], gm_ref[:, cols]
        probs = probabilities(q, k, mask)
        gp = dot(gm, v, ((1,), (1,)))
        gv_ref[:, cols] = dot(probs.astype(BF16), gm, ((0,), (0,))).astype(BF16)
        inner = jnp.sum(gp * probs, axis=-1, keepdims=True)
        gs = (probs * (gp - inner) * SCALE).astype(BF16)
        gq_ref[:, cols] = dot(gs, k, ((1,), (0,))).astype(BF16)
        gk_ref[:, cols] = dot(gs, q, ((0,), (0,))).astype(BF16)

    for step in range(2):
        head(step)
        for way, sub in ((0, 1), (1, 1), (0, 0), (1, 0)):
            gather_take(way, step, sub)
            gather_send(way, step + 1, sub)
    head(2)
    for way, sub in ((0, 1), (1, 1), (0, 0), (1, 0)):
        gather_take(way, 2, sub)
        if way == sub:
            gather_send(way, 3, sub)
    for copy in zcopies:
        copy.wait_recv()
    total = term_ref[core, x, zh].astype(F32)
    for n in range(3):
        total = total + zin_ref[n].astype(F32)
    gw_ref[...] = jnp.transpose(total).astype(BF16)
    gather_take(0, 3, 0)
    gather_take(1, 3, 1)
    for copy in pending + [swap] + xcopies + zcopies + [c for _, c in folds]:
        copy.wait_send()


def vmem():
    return pl.BlockSpec(memory_space=pltpu.VMEM)


def smem():
    return pl.BlockSpec(memory_space=pltpu.SMEM)


def params(cid):
    return pltpu.CompilerParams(collective_id=cid, has_side_effects=True, vmem_limit_bytes=48 << 20)


def sds(*shape):
    return jax.ShapeDtypeStruct(shape, BF16)


DMA = pltpu.SemaphoreType.DMA


def local(queries, key_rows, value_rows, cotangent, out_weight, patch_counts, destinations):
    slots, wt = pl.pallas_call(
        first_kernel,
        out_shape=(sds(4, SLOT, WIDTH), sds(NDP, FEAT, WIDTH)),
        in_specs=[smem(), smem()] + [vmem()] * 5,
        out_specs=(vmem(), vmem()),
        scratch_shapes=[pltpu.VMEM((ROWS, WIDTH), BF16), DMA((31,)), DMA((32,))],
        compiler_params=params(0),
        name="gather_forward",
    )(patch_counts, destinations, queries, key_rows, value_rows, cotangent, out_weight)

    def turner(turn):
        return pl.pallas_call(
            functools.partial(turn_kernel, turn),
            out_shape=sds(4, SLOT, WIDTH),
            in_specs=[vmem()],
            out_specs=vmem(),
            scratch_shapes=[DMA((4,)), DMA((4,))],
            compiler_params=params(2 + turn),
            name="turn_%d" % turn,
        )

    first = jnp.mod(-destinations[0, 0], NDP)
    index = jnp.where(first >= NDP // 2, NDP - 1 - first, first)
    turned = lax.switch(index, [turner(t) for t in range(NDP // 2)], slots)

    return pl.pallas_call(
        second_kernel,
        out_shape=(sds(DEST, OUT), sds(ROWS, WIDTH), sds(ROWS, WIDTH), sds(ROWS, WIDTH), sds(WIDTH, FEAT)),
        in_specs=[smem(), smem()] + [vmem()] * 6,
        out_specs=(vmem(),) * 5,
        scratch_shapes=[
            pltpu.VMEM((DEST, WIDTH), BF16),
            pltpu.VMEM((DEST, OUT), BF16),
            pltpu.VMEM((2, 4, 2, 32, HALF), BF16),
            pltpu.VMEM((2, 32, HALF), BF16),
            pltpu.VMEM((2, 4, 4, FEAT, WIDTH), BF16),
            pltpu.VMEM((4, 4, FEAT, WIDTH), BF16),
            pltpu.VMEM((3, 4, FEAT, WIDTH), BF16),
            pltpu.VMEM((3, FEAT, WIDTH), BF16),
            pltpu.VMEM((ROWS, WIDTH), BF16),
            DMA((2, 4, 2)), DMA((2, 4, 2)),
            DMA((2,)), DMA((2,)),
            DMA((2, 4, 2)), DMA((2, 4, 2)),
            DMA((7,)), DMA((7,)),
        ],
        compiler_params=params(1),
        name="project_backward",
    )(patch_counts, destinations, turned, queries, key_rows, value_rows, cotangent, wt)


def solution(mesh):
    in_specs = (P("dp", "mp"), P("dp", "mp"), P("dp", "mp"), P("dp", None), P("mp", "dp"), P(), P())
    out_specs = (P("dp", None), P("dp", "mp"), P("dp", "mp"), P("dp", "mp"), P("mp", "dp"))
    return jax.shard_map(local, mesh=mesh, in_specs=in_specs, out_specs=out_specs, check_vma=False)
```

time: 563 us -> 124 us (0.22)
  the two profiles are of different devices: /device:TPU:16 before, /device:TPU:2 now
where the time goes in v1:
time: 124 us; the launch traced here: 123 us
  Pallas kernels  104 us (84%)
  local copies, waits for them, and re-layouts  17.3 us (14%)
  between operations  2.04 us (2%)
    pallas_call x1, Pallas kernels, local(): pl.pallas_call(second_kernel, out_shape=(sds(DEST, OUT), sds(ROWS, WIDTH)...  63.9 us
    pallas_call x1, Pallas kernels, local(): pl.pallas_call(first_kernel, out_shape=(sds(4, SLOT, WIDTH), sds(NDP, FEA...  28.9 us
    unnamed x37, local copies, waits for them, and re-layouts  15.4 us
    pallas_call x1, Pallas kernels, local(): turned = lax.switch(index, [turner(t) for t in range(NDP // 2)], slots)  11.2 us

profile of v1, /device:TPU:2, one launch (start us, length us, event | category | flops | bytes accessed | tf_op | source)
XLA Modules:
  0.0 123.4 jit_solution(3835678485382751255)
XLA Ops:
  0.6 1.2 slice.3
  3.1 0.8 copy.15.counts_ref
  3.9 0.8 copy.16.dests_ref
  4.7 1.0 copy.14.w_ref
  5.7 0.0 copy-start
  5.7 1.4 %copy-done = bf16[256,3072]{1,0:T(8,128)(2,1)S(1)} copy-done((bf16[256,3072]{1,0:T(8,128)(2,1)S(1)}, bf16[256,3072]{1,0:T(8,128)(2,1)}, u32[]{:S(2)}) %copy-start) | copy-done | bytes 1572888
  7.1 0.0 copy-start.3
  7.1 0.9 copy-done.3
  8.0 0.0 copy-start.5
  8.0 0.9 copy-done.5
  9.0 0.0 copy-start.7
  9.0 0.9 copy-done.7
  9.9 28.9 %gather_forward.1 = (bf16[4,160,384]{2,1,0:T(8,128)(2,1)S(1)}, bf16[32,96,384]{2,1,0:T(8,128)(2,1)S(1)}) custom-call(s32[32,2]{1,0:T(8,128)S(1)} %copy.15.counts_ref, s32[32,2]{1,0:T(8,128)S(1)} %copy.16.dests_ref, bf16[320,384]{1,0:T(8,128)(2,1)S(1)} %copy-done.3, bf16[320,384]{1,0:T(8,128)(2,1)S(1)} %copy-done.5, bf16[320,384]{1,0:T(8,128)(2,1)S(1)} %copy-done.7, ...), custom_call_target="tpu_custom_call" | custom-call | tf_op jit(solution)/shard_map/gather_forward/pallas_call | solution.py:396
  38.8 0.0 copy-start.2
  38.8 1.4 %copy-done.2 = bf16[32,96,384]{2,1,0:T(8,128)(2,1)} copy-done((bf16[32,96,384]{2,1,0:T(8,128)(2,1)}, bf16[32,96,384]{2,1,0:T(8,128)(2,1)S(1)}, u32[]{:S(2)}) %copy-start.2) | copy-done | bytes 2359320
  40.2 0.0 copy-start.1
  40.2 0.0 copy-start.4
  40.2 11.2 %conditional.1 = (bf16[4,160,384]{2,1,0:T(8,128)(2,1)}) conditional(s32[]{:T(128)} %clamp.3, bf16[4,160,384]{2,1,0:T(8,128)(2,1)S(1)} %get-tuple-element.40, bf16[4,160,384]{2,1,0:T(8,128)(2,1)S(1)} %get-tuple-element.40, bf16[4,160,384]{2,1,0:T(8,128)(2,1)S(1)} %get-tuple-element.40, ...), branch_computations={%region_0.1_spmd, %region_1.2_spmd, %region_2.3_spmd, %region_3.4_... | conditional | bytes 8 | solution.py:419
  40.2 11.2 %turn_1.1 = bf16[4,160,384]{2,1,0:T(8,128)(2,1)} custom-call(bf16[4,160,384]{2,1,0:T(8,128)(2,1)S(1)} %in_ref.1), custom_call_target="tpu_custom_call" | custom-call | tf_op jit(solution)/shard_map/cond/branch_1_fun/turn_1/pallas_call | solution.py:419
  51.5 0.0 copy-done.1
  51.5 0.0 copy-done.4
  51.5 0.0 copy-start.6
  51.5 0.9 copy-done.6
  52.4 0.0 copy-start.8
  52.5 0.9 copy-done.8
  53.4 63.9 %project_backward.1 = (bf16[256,3072]{1,0:T(8,128)(2,1)S(1)}, bf16[320,384]{1,0:T(8,128)(2,1)S(1)}, bf16[320,384]{1,0:T(8,128)(2,1)S(1)}, bf16[320,384]{1,0:T(8,128)(2,1)S(1)}, bf16[384,96]{1,0:T(8,128)(2,1)S(1)}) custom-call(s32[32,2]{1,0:T(8,128)S(1)} %copy.15.counts_ref, s32[32,2]{1,0:T(8,128)S(1)} %copy.16.dests_ref, ...), custom_call_target="tpu_custom_call" | custom-call | tf_op jit(solution)/shard_map/project_backward/pallas_call | solution.py:421
  117.3 0.0 copy-start.9
  117.3 0.7 copy-done.9
  118.0 0.0 copy-start.11
  118.0 0.7 copy-done.11
  118.7 0.0 copy-start.13
  118.7 0.7 copy-done.13
  119.4 0.7 copy.17
  120.1 0.0 copy-start.14
  120.1 0.0 copy-start.12
  120.1 0.0 copy-start.10
  120.1 1.1 copy.38
  121.3 0.0 copy-done.14
  121.3 0.7 copy.39
  122.0 0.0 copy-done.12
  122.0 0.7 copy.40
  122.7 0.0 copy-done.10
  122.7 0.7 copy.41
Async XLA Ops:
  5.7 1.4 %copy-start = (bf16[256,3072]{1,0:T(8,128)(2,1)S(1)}, bf16[256,3072]{1,0:T(8,128)(2,1)}, u32[]{:S(2)}) copy-start(bf16[256,3072]{1,0:T(8,128)(2,1)} %cot_ref.3) | copy-start | bytes 4718596
  7.1 0.9 copy-start.3
  8.0 0.9 copy-start.5
  9.0 0.9 copy-start.7
  38.8 1.4 %copy-start.2 = (bf16[32,96,384]{2,1,0:T(8,128)(2,1)}, bf16[32,96,384]{2,1,0:T(8,128)(2,1)S(1)}, u32[]{:S(2)}) copy-start(bf16[32,96,384]{2,1,0:T(8,128)(2,1)S(1)} %get-tuple-element.41.wt_ref) | copy-start | bytes 7077892
  40.2 11.2 %copy-start.1 = (bf16[256,3072]{1,0:T(8,128)(2,1)S(1)}, bf16[256,3072]{1,0:T(8,128)(2,1)}, u32[]{:S(2)}) copy-start(bf16[256,3072]{1,0:T(8,128)(2,1)} %cot_ref.3) | copy-start | bytes 4718596
  40.2 11.3 %copy-start.4 = (bf16[320,384]{1,0:T(8,128)(2,1)S(1)}, bf16[320,384]{1,0:T(8,128)(2,1)}, u32[]{:S(2)}) copy-start(bf16[320,384]{1,0:T(8,128)(2,1)} %q_ref.3) | copy-start | bytes 737284
  51.5 0.9 copy-start.6
  52.4 0.9 copy-start.8
  117.3 0.7 copy-start.9
  118.0 0.7 copy-start.11
  118.7 0.7 copy-start.13
  120.1 1.2 copy-start.14
  120.1 1.9 %copy-start.12 = (bf16[320,384]{1,0:T(8,128)(2,1)S(1)}, bf16[320,384]{1,0:T(8,128)(2,1)}, u32[]{:S(2)}) copy-start(bf16[320,384]{1,0:T(8,128)(2,1)} %copy-done.11) | copy-start | bytes 737284
  120.1 2.6 %copy-start.10 = (bf16[320,384]{1,0:T(8,128)(2,1)S(1)}, bf16[320,384]{1,0:T(8,128)(2,1)}, u32[]{:S(2)}) copy-start(bf16[320,384]{1,0:T(8,128)(2,1)} %copy-done.9) | copy-start | bytes 737284
